TPU v7x, 128 devices: a whole 4x4x4 slice. The times are simulated.
128 devices in a mesh: row: 8 (over x, core), col: 16 (over z, y).
Axes of the slice: x: 4, y: 4, z: 4, core: 2. Of those that a mesh axis runs over, the one named last changes fastest.
Arguments:
- object_field: float32 [2, 4096, 8192], P(None, 'row', 'col'), may hold values from -11 to 11
- probe_modes: float32 [2, 2, 256, 256], replicated, may hold values from -4 to 4
- intensities: float32 [256, 256, 256], P(('row', 'col')), may hold values from 0.05 to 5
- positions: int32 [256, 2], replicated, may hold values from 0 to 8191, as said below
- counts: int32 [128], replicated, may hold values from 1 to 2, as said below
Outputs:
- new_object: float32 [2, 4096, 8192], P(None, 'row', 'col')
- new_probe: float32 [2, 2, 256, 256], replicated
Inputs may be any that keep to these rules, and one draw needn't show every extreme that they name: Device d (devices numbered row by row over the mesh) holds its counts[d] patterns in its first counts[d] slots, slots d * 2 onward; its other slots are empty. Some device is full in every draw. `positions`: slot s belongs to device d = s div 2, in mesh row r and column c; its patch's top-left pixel lies in that device's tile, rows r * 512 to (r + 1) * 512 - 1 and columns c * 512 to (c + 1) * 512 - 1. In every draw some live slot sits at its tile's last row and last column.
All inputs are finite; a program needn't handle non-finite values.
Results may differ from a plain program's by a relative error of at most 0.00011.
Values sent between devices are 32-bit elements; how exact they have to be, the bound alone decides.
A program may use at most 192 MiB of HBM per device.

v0:
```python
import functools
import math

import jax
import jax.numpy as jnp
import ml_dtypes
import numpy as np
from jax import lax
from jax.experimental import pallas as pl
from jax.experimental.pallas import tpu as pltpu
from jax.sharding import PartitionSpec as P

ITERS = 3
M = 256
H = 128
T = 512
MODEL_FLOOR = 0.5
DAMPING = 0.2
SMALL = 1e-06
MESH = pl.DeviceIdType.MESH
F32 = jnp.float32
BF16 = jnp.bfloat16


def tables():
    k = np.arange(H)
    angle = 2.0 * np.pi * ((k[:, None] * k[None, :]) % H) / H
    c, s = np.cos(angle) / 16.0, np.sin(angle) / 16.0

    def three(matrix, axis):
        wide = matrix.astype(np.float32)
        hi = wide.astype(ml_dtypes.bfloat16)
        lo = (wide - hi.astype(np.float32)).astype(ml_dtypes.bfloat16)
        return np.concatenate([hi, hi, lo], axis=axis)

    left = np.block([[c, s], [-s, c]])
    left_back = np.block([[c, -s], [s, c]])
    turn = 2.0 * np.pi * k / M
    rows = np.stack([np.cos(turn), np.sin(turn)])[:, :, None] * np.ones((1, 1, H))
    cols = rows.transpose(0, 2, 1)[:, :16]
    order = np.concatenate([np.arange(0, M, 2), np.arange(1, M, 2)])
    pick = np.zeros((M, M), np.float32)
    pick[np.arange(M), order] = 1.0
    return (
        three(left, 1),
        three(left_back, 1),
        three(left.T, 0),
        three(left_back.T, 0),
        rows.astype(np.float32),
        cols.astype(np.float32),
        pick.astype(ml_dtypes.bfloat16),
        np.ascontiguousarray(pick.T).astype(ml_dtypes.bfloat16),
    )


def dot(a, b):
    return jnp.dot(a, b, preferred_element_type=F32)


def cat(parts, axis):
    return jnp.concatenate(parts, axis=axis)


def split(x):
    hi = x.astype(BF16)
    lo = (x - hi.astype(F32)).astype(BF16)
    return hi, lo


def store_parts(ref, k, row, lane, axis, x):
    hi, lo = split(x)
    for n, part in enumerate((hi, lo, hi)):
        r, c = (row + n * M, lane) if axis == 0 else (row, lane + n * M)
        ref[k, r:r + 16, c:c + H] = part


class Stream:
    def __init__(self, rows, axes, sizes):
        self.half = rows // 2
        self.axes = axes
        self.n = [sizes[a] for a in axes]
        self.r1 = self.half // self.n[0]
        self.r2 = self.r1 // self.n[1]

    def scratch(self):
        vm = lambda *shape: pltpu.VMEM(shape, F32)
        n1, n2, n3 = self.n
        return [
            vm(2, self.half, H),
            vm(ITERS, self.half, H),
            vm(self.half, H),
            vm(ITERS, n1, self.r1, H),
            vm(self.r1, H),
            vm(ITERS, n2, self.r2, H),
            vm(self.r2, H),
            vm(ITERS, n3, self.r2, H),
            vm(ITERS, self.r1, H),
            vm(ITERS, self.half, H),
            vm(ITERS, 2, self.half, H),
            pltpu.SemaphoreType.DMA((ITERS, 7, 4)),
            pltpu.SemaphoreType.DMA((ITERS, 7, 4)),
        ]


def kernel(
    rows_n, cols_n, nz, ny, streams,
    pos, counts, obj_in, probe_in, meas_in, wl_in, wlb_in, wr_in, wrb_in, twr_in, twc_in, pick_in,
    pick_t_in, obj_out, probe,
    meas, wl, wlb, wr, wrb, twr, twc, pick, pick_t,
    obj, acc, den, zbuf, cbuf, power, patch, exits, lop, lout, rop, rout, root, upd, out_up,
    hr, hl, vu, vh,
    load_sem, io_sem, hs, hrs, vs, vrs, us, urs, *ar,
):
    nx = rows_n // 2
    row, col = lax.axis_index("row"), lax.axis_index("col")
    core, xi = lax.rem(row, 2), lax.div(row, 2)
    yi, zi = lax.rem(col, ny), lax.div(col, ny)
    me = {"x": xi, "y": yi, "z": zi}
    size = {"x": nx, "y": ny, "z": nz}

    def device(axis, j):
        if axis == "x":
            return (j * 2 + core, col)
        if axis == "y":
            return (row, zi * ny + j)
        return (row, j * ny + yi)

    partner = (row + 1 - 2 * core, col)
    not_left, not_right = col > 0, col < cols_n - 1
    not_top, not_bottom = row > 0, row < rows_n - 1

    loads = []
    for ch in range(2):
        for b in range(4):
            load = pltpu.make_async_copy(
                obj_in.at[ch, :, pl.ds(b * H, H)], obj.at[ch, b, pl.ds(M, T), :], io_sem.at[ch, b]
            )
            load.start()
            loads.append(load)
    later = []
    for i, (src, dst) in enumerate(
        (
            (meas_in, meas), (pick_in, pick), (pick_t_in, pick_t), (probe_in, probe), (wl_in, wl),
            (wlb_in, wlb), (wr_in, wr), (wrb_in, wrb), (twr_in, twr), (twc_in, twc),
        )
    ):
        load = pltpu.make_async_copy(src, dst, load_sem.at[i])
        load.start()
        later.append(load)

    barrier = pltpu.get_barrier_semaphore()

    def greet(who):
        pl.semaphore_signal(barrier, inc=1, device_id=who, device_id_type=MESH)

    greet(partner)
    peers = 1
    for axis in ("z", "y", "x"):
        for d in range(1, size[axis]):
            greet(device(axis, lax.rem(me[axis] + d, size[axis])))
            peers += 1
    pl.when(not_left)(lambda: greet((row, col - 1)))
    pl.when(not_right)(lambda: greet((row, col + 1)))
    pl.when(not_top)(lambda: greet((row - 1, col)))
    pl.when(not_bottom)(lambda: greet((row + 1, col)))

    zbuf[...] = jnp.zeros_like(zbuf)
    cbuf[...] = jnp.zeros_like(cbuf)

    @pl.when(jnp.logical_not(not_left))
    def _():
        hl[...] = jnp.zeros_like(hl)

    @pl.when(jnp.logical_not(not_right))
    def _():
        hr[...] = jnp.zeros_like(hr)

    @pl.when(jnp.logical_not(not_top))
    def _():
        vu[...] = jnp.zeros_like(vu)

    @pl.when(jnp.logical_not(not_bottom))
    def _():
        vh[...] = jnp.zeros_like(vh)

    for load in loads:
        load.wait()
    pl.semaphore_wait(
        barrier,
        peers
        + not_left.astype(jnp.int32) + not_right.astype(jnp.int32)
        + not_top.astype(jnp.int32) + not_bottom.astype(jnp.int32),
    )

    def remote(src, dst, send, recv, who):
        return pltpu.make_async_remote_copy(
            src_ref=src, dst_ref=dst, send_sem=send, recv_sem=recv, device_id=who, device_id_type=MESH
        )

    def to_left(src, turn, ch, q):
        base = M if src is obj else 0
        return remote(
            src.at[ch, pl.ds(0, 2), pl.ds(base + q * H, H), :], hr.at[turn, ch, q],
            hs.at[turn, 0, ch, q], hrs.at[turn, 0, ch, q], (row, col - 1),
        )

    def to_right(turn, ch, q):
        return remote(
            acc.at[ch, pl.ds(4, 2), pl.ds(q * H, H), :], hl.at[turn, ch, q],
            hs.at[turn, 1, ch, q], hrs.at[turn, 1, ch, q], (row, col + 1),
        )

    def down(it, s, ch):
        return remote(
            upd.at[s, ch], vu.at[it, s, ch], us.at[it, s, ch], urs.at[it, s, ch], (row + 1, col)
        )

    def up(turn, s, ch):
        return remote(
            out_up.at[s, ch], vh.at[turn, s, ch], vs.at[turn, s, ch], vrs.at[turn, s, ch],
            (row - 1, col),
        )

    C = 64
    lane = lax.broadcasted_iota(jnp.int32, (C, H), 1)
    line = lax.broadcasted_iota(jnp.int32, (C, H), 0)

    def place_of(dr, dc, s):
        r, c = row + dr, col + dc
        there = (r >= 0) & (r < rows_n) & (c >= 0) & (c < cols_n)
        r, c = jnp.clip(r, 0, rows_n - 1), jnp.clip(c, 0, cols_n - 1)
        dev = r * cols_n + c
        y = jnp.clip(pos[0, dev * 2 + s] - r * T, 0, T - 1)
        x = jnp.clip(pos[1, dev * 2 + s] - c * T, 0, T - 1)
        live = jnp.where(there & (s < counts[dev]), 1.0, 0.0).astype(F32)
        return y, x, live

    def extract(ch, start, x, store):
        q, r = lax.div(x, H), lax.rem(x, H)
        back = lax.rem(H - r, H)
        keep = lane < H - r
        for i in range(0, M, C):
            b = [pltpu.roll(obj[ch, q + j, pl.ds(start + i, C), :], back, 1) for j in range(3)]
            store(i, jnp.where(keep, b[0], b[1]), jnp.where(keep, b[1], b[2]))

    def spread(z, load, x):
        r = lax.rem(x, H)
        keep = lane >= r
        for i in range(0, M, C):
            u0, u1 = load(i)
            a, b = pltpu.roll(u0, r, 1), pltpu.roll(u1, r, 1)
            z[0, T + i:T + i + C, :] = jnp.where(keep, a, 0.0)
            z[1, T + i:T + i + C, :] = jnp.where(keep, b, a)
            z[2, T + i:T + i + C, :] = jnp.where(keep, 0.0, b)

    def add_placed(z, dst, blocks, dr, dc, y, x, weight):
        q = lax.div(x, H) + 4 * dc
        length = T if dr == 0 else M
        start = T - y - dr * T
        if dr != 0:
            start = jnp.minimum(start, 3 * M)
        for b in blocks:
            j = b - q
            inside = jnp.where((j >= 0) & (j <= 2), weight, 0.0).astype(F32)
            near = jnp.clip(j, 0, 2)
            for i in range(0, length, C):
                dst[b, i:i + C, :] += z[near, pl.ds(start + i, C), :] * inside

    def send_up(turn, ch):
        for s in range(2):
            y, x, _ = place_of(-1, 0, s)

            def store(i, b0, b1, s=s):
                out_up[s, ch, 0, i:i + C, :] = b0
                out_up[s, ch, 1, i:i + C, :] = b1

            extract(ch, jnp.maximum(y - T, -M) + M, x, store)
            pl.when(not_top)(lambda: up(turn, s, ch).start())

    first = [(ch, q) for half in range(2) for ch in range(2) for q in (2 * half, 2 * half + 1)]

    def first_piece(n):
        pl.when(not_left)(lambda: to_left(obj, 0, *first[n]).start())

    first_piece(0)
    first_piece(1)

    for load in later:
        load.wait()

    for s in range(2):
        value = meas[s]
        for step in range(2):
            h = value.astype(BF16)
            rest = value - h.astype(F32)
            m = rest.astype(BF16)
            low = (rest - m.astype(F32)).astype(BF16)
            if step == 0:
                value = (dot(pick[...], h) + dot(pick[...], m)) + dot(pick[...], low)
            else:
                value = (dot(h, pick_t[...]) + dot(m, pick_t[...])) + dot(low, pick_t[...])
        root[s] = jnp.sqrt(value)

    for n, (ch, q) in enumerate(first):
        pl.when(not_right)(lambda: to_left(obj, 0, ch, q).wait_recv())
        if n + 2 < len(first):
            first_piece(n + 2)
        for b in range(2):
            for i in range(0, H, C):
                obj[ch, 4 + b, M + q * H + i:M + q * H + i + C, :] = hr[0, ch, q, b, i:i + C, :]
        if q == 1:
            send_up(0, ch)

    def take(it, s):
        y, x, live = place_of(0, 0, s)

        def store(i, b0, b1, ch):
            own = line + i < T - y
            parts = (b0, b1)
            for b in range(2):
                value = jnp.where(own, parts[b], vh[it, s, ch, b, i:i + C, :])
                patch[s, ch, i:i + C, b * H:(b + 1) * H] = value
                sum_ref(2, 0, b)[i:i + C, :] += value * value * live

        for ch in range(2):
            extract(ch, M + y, x, functools.partial(store, ch=ch))

    def slot(it, s):
        _, _, live = place_of(0, 0, s)
        cc, sc = twc[0], twc[1]
        lanes = (slice(0, H), slice(H, M))
        for k in range(2):
            for i in range(0, H, 16):
                cr, sr = twr[0, i:i + 16, :], twr[1, i:i + 16, :]
                for b in range(2):
                    er, ei = [], []
                    for t in (i, i + H):
                        at = (slice(t, t + 16), lanes[b])
                        pr, pi = patch[(s, 0) + at], patch[(s, 1) + at]
                        qr, qi = probe[(0, k) + at], probe[(1, k) + at]
                        er.append(qr * pr - qi * pi)
                        ei.append(qr * pi + qi * pr)
                        exits[(k, 0) + at] = er[-1]
                        exits[(k, 1) + at] = ei[-1]
                    dr, di = er[0] - er[1], ei[0] - ei[1]
                    store_parts(lop, k, i, b * H, 0, er[0] + er[1])
                    store_parts(lop, k, i + H, b * H, 0, ei[0] + ei[1])
                    store_parts(lop, k, i, M + b * H, 0, dr * cr + di * sr)
                    store_parts(lop, k, i + H, M + b * H, 0, di * cr - dr * sr)
            lout[k] = dot(wl[...], lop[k])
        for k in range(2):
            for i in range(0, M, 16):
                j, c = i % H, (i // H) * M
                lr = [lout[k, j:j + 16, c + b * H:c + b * H + H] for b in range(2)]
                li = [lout[k, j + H:j + H + 16, c + b * H:c + b * H + H] for b in range(2)]
                dr, di = lr[0] - lr[1], li[0] - li[1]
                store_parts(rop, k, i, 0, 1, lr[0] + lr[1])
                store_parts(rop, k, i, H, 1, li[0] + li[1])
                store_parts(rop, k, i + M, 0, 1, dr * cc + di * sc)
                store_parts(rop, k, i + M, H, 1, di * cc - dr * sc)
            rout[k] = dot(rop[k], wr[...])
        for i in range(0, 2 * M, 16):
            f = [[rout[k, i:i + 16, lanes[b]] for b in range(2)] for k in range(2)]
            model = (f[0][0] * f[0][0] + f[0][1] * f[0][1]) + (f[1][0] * f[1][0] + f[1][1] * f[1][1])
            scale = root[s, i % M:i % M + 16, lanes[i // M]]
            scale = scale * lax.rsqrt(jnp.maximum(model, MODEL_FLOOR))
            for k in range(2):
                for b in range(2):
                    store_parts(rop, k, i, b * H, 1, f[k][b] * scale)
        for k in range(2):
            rout[k] = dot(rop[k], wrb[...])
        for k in range(2):
            for i in range(0, M, 16):
                er, ei = rout[k, i:i + 16, lanes[0]], rout[k, i:i + 16, lanes[1]]
                dr, di = rout[k, i + M:i + M + 16, lanes[0]], rout[k, i + M:i + M + 16, lanes[1]]
                tr, ti = dr * cc - di * sc, di * cc + dr * sc
                j, c = i % H, (i // H) * M
                store_parts(lop, k, j, c, 0, er + tr)
                store_parts(lop, k, j, c + H, 0, er - tr)
                store_parts(lop, k, j + H, c, 0, ei + ti)
                store_parts(lop, k, j + H, c + H, 0, ei - ti)
            lout[k] = dot(wlb[...], lop[k])
        for i in range(0, H, 16):
            cr, sr = twr[0, i:i + 16, :], twr[1, i:i + 16, :]
            for b in range(2):
                u = [[None, None], [None, None]]
                for k in range(2):
                    c = b * H
                    er, ei = lout[k, i:i + 16, c:c + H], lout[k, i + H:i + H + 16, c:c + H]
                    dr = lout[k, i:i + 16, M + c:M + c + H]
                    di = lout[k, i + H:i + H + 16, M + c:M + c + H]
                    tr, ti = dr * cr - di * sr, di * cr + dr * sr
                    for n, (gr, gi) in enumerate(((er + tr, ei + ti), (er - tr, ei - ti))):
                        t = i + n * H
                        at = (slice(t, t + 16), lanes[b])
                        gr = (gr - exits[(k, 0) + at]) * live
                        gi = (gi - exits[(k, 1) + at]) * live
                        qr, qi = probe[(0, k) + at], probe[(1, k) + at]
                        pr, pi = patch[(s, 0) + at], patch[(s, 1) + at]
                        ur, ui = qr * gr + qi * gi, qr * gi - qi * gr
                        if k == 0:
                            u[n] = [ur, ui]
                        else:
                            upd[s, 0, b, t:t + 16, :] = u[n][0] + ur
                            upd[s, 1, b, t:t + 16, :] = u[n][1] + ui
                        sum_ref(k, 0, b)[t:t + 16, :] += pr * gr + pi * gi
                        sum_ref(k, 1, b)[t:t + 16, :] += pr * gi - pi * gr
        for ch in range(2):
            pl.when(not_bottom)(lambda: down(it, s, ch).start())

    def place(ch, dr, s, src):
        y, x, _ = place_of(dr, 0, s)
        spread(zbuf.at[ch], lambda i: (src[0, i:i + C, :], src[1, i:i + C, :]), x)
        add_placed(zbuf.at[ch], acc.at[ch], range(6), dr, 0, y, x, 1.0)

    def sum_ref(k, part, b):
        if k == 2:
            return ar[26].at[b]
        return ar[13 * k].at[part, pl.ds(b * M, M), :]

    def group(it, n, phase, axis, src, dst):
        ssem, rsem = ar[13 * n + 11], ar[13 * n + 12]
        out = []
        for d in range(1, size[axis]):
            j = lax.rem(me[axis] + d, size[axis])
            out.append(
                remote(src(j), dst, ssem.at[it, phase, d], rsem.at[it, phase, d], device(axis, j))
            )
        return out

    def phase_copies(it, n, phase):
        st = streams[n]
        own, cin, m0, r1, m1, r2, m2, r3, g2, g1, gc, ssem, rsem = ar[13 * n:13 * n + 13]
        a, b, c = st.axes
        R1, R2 = st.r1, st.r2
        rows_of = lambda j, r: pl.ds(pl.multiple_of(j * r, 8), r)
        if phase == 0:
            return [remote(own.at[1 - core], cin.at[it], ssem.at[it, 0, 0], rsem.at[it, 0, 0], partner)]
        if phase == 1:
            return group(it, n, 1, a, lambda j: m0.at[rows_of(j, R1), :], r1.at[it, me[a]])
        if phase == 2:
            return group(it, n, 2, b, lambda j: m1.at[rows_of(j, R2), :], r2.at[it, me[b]])
        if phase == 3:
            return group(it, n, 3, c, lambda j: m2, r3.at[it, me[c]])
        if phase == 4:
            part = g2.at[it, rows_of(me[b], R2), :]
            return group(it, n, 4, b, lambda j: part, part)
        if phase == 5:
            part = g1.at[it, rows_of(me[a], R1), :]
            return group(it, n, 5, a, lambda j: part, part)
        part = gc.at[it, core]
        return [remote(part, part, ssem.at[it, 6, 0], rsem.at[it, 6, 0], partner)]

    def ar_start(it, which):
        for n in which:
            for copy in phase_copies(it, n, 0):
                copy.start()

    def ar_step(it, which, phase):
        for n in which:
            st = streams[n]
            own, cin, m0, r1, m1, r2, m2, r3, g2, g1, gc, ssem, rsem = ar[13 * n:13 * n + 13]
            a, b, c = st.axes
            rows_of = lambda j, r: pl.ds(pl.multiple_of(j * r, 8), r)
            for copy in phase_copies(it, n, phase):
                copy.wait_recv()
            if phase == 0:
                for i in range(0, st.half, C):
                    m0[i:i + C, :] = own[core, i:i + C, :] + cin[it, i:i + C, :]
                r1[it, me[a]] = m0[rows_of(me[a], st.r1), :]
            elif phase == 1:
                m1[...] = functools.reduce(lambda p, q: p + q, [r1[it, j] for j in range(st.n[0])])
                r2[it, me[b]] = m1[rows_of(me[b], st.r2), :]
            elif phase == 2:
                m2[...] = functools.reduce(lambda p, q: p + q, [r2[it, j] for j in range(st.n[1])])
                r3[it, me[c]] = m2[...]
            elif phase == 3:
                g2[it, rows_of(me[b], st.r2), :] = functools.reduce(
                    lambda p, q: p + q, [r3[it, j] for j in range(st.n[2])]
                )
            elif phase == 4:
                g1[it, rows_of(me[a], st.r1), :] = g2[it]
            elif phase == 5:
                gc[it, core] = g1[it]
            if phase < 6:
                for copy in phase_copies(it, n, phase + 1):
                    copy.start()

    mode_sums, power_sum = (0, 1), (2,)

    def iteration(it, _):
        more = it < ITERS - 1
        send_left = not_left & more
        get_right = not_right & more
        acc[...] = jnp.zeros_like(acc)
        for n in range(3):
            ar[13 * n][...] = jnp.zeros_like(ar[13 * n])

        for s in range(2):
            take(it, s)
        ar_start(it, power_sum)

        def one(s, carry):
            slot(it, s)

            @pl.when(s == 0)
            def _():
                ar_step(it, power_sum, 0)

            return carry

        lax.fori_loop(0, 2, one, 0)
        ar_start(it, mode_sums)

        def send(ch, q):
            pl.when(not_right)(lambda: to_right(it, ch, q).start())
            pl.when(send_left)(lambda: to_left(acc, it + 1, ch, q).start())

        def arrive(ch, q):
            pl.when(not_left)(lambda: to_right(it, ch, q).wait_recv())
            pl.when(get_right)(lambda: to_left(acc, it + 1, ch, q).wait_recv())

        def update(ch, q):
            for i in range(q * H, q * H + H, C):
                rows, there, j = slice(i, i + C), slice(M + i, M + i + C), i - q * H
                for b in range(4):
                    step = acc[ch, b, rows, :]
                    if b < 2:
                        step = step + hl[it, ch, q, b, j:j + C, :]
                    obj[ch, b, there, :] += step * den[b, rows, :]

            @pl.when(get_right)
            def _():
                for i in range(q * H, q * H + H, C):
                    rows, there, j = slice(i, i + C), slice(M + i, M + i + C), i - q * H
                    for b in range(2):
                        step = acc[ch, 4 + b, rows, :] + hr[it + 1, ch, q, b, j:j + C, :]
                        obj[ch, 4 + b, there, :] += step * den[4 + b, rows, :]

        def below(s, ch):
            pl.when(not_top)(lambda: down(it, s, ch).wait_recv())
            place(ch, -1, s, vu.at[it, s, ch])

        for ch in range(2):
            for s in range(2):
                place(ch, 0, s, upd.at[s, ch])
            if ch == 0:
                send(0, 2)
                send(0, 3)
        ar_step(it, power_sum, 1)
        ar_step(it, mode_sums, 0)
        for q in range(2):
            if q == 0:
                below(0, 0)
                below(1, 0)
            arrive(0, 2 + q)
            send(0, q)
        below(0, 1)
        below(1, 1)
        ar_step(it, power_sum, 2)

        power_all = jnp.zeros((C, H), F32)
        for b in range(2):
            for i in range(0, M, C):
                at = (slice(i, i + C), slice(b * H, b * H + H))
                square = (
                    probe[(0, 0) + at] ** 2 + probe[(1, 0) + at] ** 2
                    + probe[(0, 1) + at] ** 2 + probe[(1, 1) + at] ** 2
                )
                power[b, i:i + C, :] = square
                power_all = power_all + square
        reg_object = DAMPING * (jnp.sum(power_all) * (1.0 / (M * M))) + SMALL
        den[...] = jnp.zeros_like(den)
        for dr in (0, -1):
            for dc, blocks in ((0, range(6)), (-1, range(2)), (1, range(4, 6))):

                def cover(s, carry, dr=dr, dc=dc, blocks=blocks):
                    y, x, live = place_of(dr, dc, s)
                    spread(cbuf, lambda i: (power[0, i:i + C, :], power[1, i:i + C, :]), x)
                    add_placed(cbuf, den, blocks, dr, dc, y, x, live)
                    return carry

                lax.fori_loop(0, 2, cover, 0)
        for b in range(6):
            for i in range(0, T, C):
                den[b, i:i + C, :] = 1.0 / (den[b, i:i + C, :] + reg_object)

        arrive(0, 0)
        send(1, 0)
        update(0, 0)
        ar_step(it, mode_sums, 1)
        arrive(0, 1)
        send(1, 1)
        update(0, 1)
        pl.when(more)(lambda: send_up(it + 1, 0))
        ar_step(it, power_sum, 3)
        ar_step(it, mode_sums, 2)
        arrive(1, 0)
        send(1, 2)
        update(1, 0)
        ar_step(it, mode_sums, 3)
        arrive(1, 1)
        send(1, 3)
        update(1, 1)
        pl.when(more)(lambda: send_up(it + 1, 1))
        update(0, 2)
        update(0, 3)
        ar_step(it, power_sum, 4)
        ar_step(it, mode_sums, 4)
        arrive(1, 2)
        update(1, 2)
        ar_step(it, power_sum, 5)
        ar_step(it, mode_sums, 5)
        arrive(1, 3)
        update(1, 3)
        for n in range(len(streams)):
            for copy in phase_copies(it, n, 6):
                copy.wait_recv()

        def total(k, part, b, i):
            if k == 2:
                return ar[36][it, b, i:i + C, :]
            return ar[13 * k + 10][it, part, b * M + i:b * M + i + C, :]

        sums = jnp.zeros((C, H), F32)
        for b in range(2):
            for i in range(0, M, C):
                sums = sums + total(2, 0, b, i)
        reg_probe = DAMPING * (jnp.sum(sums) * (1.0 / (M * M))) + SMALL
        for b in range(2):
            for i in range(0, M, C):
                scale = 1.0 / (total(2, 0, b, i) + reg_probe)
                for k in range(2):
                    for part in range(2):
                        at = (part, k, slice(i, i + C), slice(b * H, b * H + H))
                        probe[at] += total(k, part, b, i) * scale

        for n in range(len(streams)):
            for phase in range(7):
                for copy in phase_copies(it, n, phase):
                    copy.wait_send()
        for ch in range(2):
            for q in range(4):
                pl.when(not_right)(lambda: to_right(it, ch, q).wait_send())
                pl.when(send_left)(lambda: to_left(acc, it + 1, ch, q).wait_send())
            for s in range(2):
                pl.when(not_bottom)(lambda: down(it, s, ch).wait_send())
                pl.when(not_bottom & more)(lambda: up(it + 1, s, ch).wait_recv())
                pl.when(not_top & more)(lambda: up(it + 1, s, ch).wait_send())
        return 0

    for ch in range(2):
        for q in range(4):
            pl.when(not_left)(lambda: to_left(obj, 0, ch, q).wait_send())
        for s in range(2):
            pl.when(not_bottom)(lambda: up(0, s, ch).wait_recv())
            pl.when(not_top)(lambda: up(0, s, ch).wait_send())

    lax.fori_loop(0, ITERS, iteration, 0)

    stores = []
    for ch in range(2):
        for b in range(4):
            store = pltpu.make_async_copy(
                obj.at[ch, b, pl.ds(M, T), :], obj_out.at[ch, :, pl.ds(b * H, H)], io_sem.at[ch, b]
            )
            store.start()
            stores.append(store)
    for store in stores:
        store.wait()


def shards(rows_n, cols_n, nz, ny, object_field, probe_modes, intensities, positions, counts):
    sizes = {"x": rows_n // 2, "y": ny, "z": nz}
    streams = (
        Stream(1024, ("x", "z", "y"), sizes),
        Stream(1024, ("x", "y", "z"), sizes),
        Stream(512, ("x", "z", "y"), sizes),
    )
    vm = lambda *shape: pltpu.VMEM(shape, F32)
    sem = lambda *shape: pltpu.SemaphoreType.DMA(shape)
    consts = [jnp.asarray(t) for t in tables()]
    scratch = [vm(2, M, M)] + [pltpu.VMEM(t.shape, t.dtype) for t in consts]
    scratch += [
        vm(2, 6, 1024, H),
        vm(2, 6, T, H),
        vm(6, T, H),
        vm(2, 3, 1024, H),
        vm(3, 1024, H),
        vm(2, M, H),
        vm(2, 2, M, M),
        vm(2, 2, M, M),
        pltpu.VMEM((2, 3 * M, 2 * M), BF16),
        vm(2, M, 2 * M),
        pltpu.VMEM((2, 2 * M, 3 * M), BF16),
        vm(2, 2 * M, M),
        vm(2, M, M),
        vm(2, 2, 2, M, H),
        vm(2, 2, 2, M, H),
        vm(ITERS, 2, 4, 2, H, H),
        vm(ITERS, 2, 4, 2, H, H),
        vm(ITERS, 2, 2, 2, M, H),
        vm(ITERS, 2, 2, 2, M, H),
        sem(10),
        sem(2, 4),
        sem(ITERS, 2, 2, 4),
        sem(ITERS, 2, 2, 4),
        sem(ITERS, 2, 2),
        sem(ITERS, 2, 2),
        sem(ITERS, 2, 2),
        sem(ITERS, 2, 2),
    ]
    for st in streams:
        scratch += st.scratch()
    smem = pl.BlockSpec(memory_space=pltpu.SMEM)
    vmem = pl.BlockSpec(memory_space=pltpu.VMEM)
    hbm = pl.BlockSpec(memory_space=pl.ANY)
    return pl.pallas_call(
        functools.partial(kernel, rows_n, cols_n, nz, ny, streams),
        out_shape=(
            jax.ShapeDtypeStruct((2, T, T), F32),
            jax.ShapeDtypeStruct((2, 2, M, M), F32),
        ),
        in_specs=[smem, smem, hbm, hbm, hbm] + [hbm] * len(consts),
        out_specs=(hbm, vmem),
        scratch_shapes=scratch,
        compiler_params=pltpu.CompilerParams(
            collective_id=0, has_side_effects=True, vmem_limit_bytes=62 * 1024 * 1024
        ),
        name="ptycho",
    )(positions.T, counts, object_field, probe_modes, intensities, *consts)


def solution(mesh):
    rows_n, cols_n = mesh.shape["row"], mesh.shape["col"]
    ny = math.isqrt(cols_n)
    nz = cols_n // ny
    placed = (P(None, "row", "col"), P(), P(("row", "col"), None, None), P(), P())
    return jax.shard_map(
        functools.partial(shards, rows_n, cols_n, nz, ny),
        mesh=mesh,
        in_specs=placed,
        out_specs=(P(None, "row", "col"), P()),
        check_vma=False,
    )
```

profile of v0, /device:TPU:1, one launch (start us, length us, event | category | flops | bytes accessed | tf_op | source)
XLA Modules:
  0.0 196.7 jit_solution(16773085989225638070)
XLA Ops:
  0.6 191.9 %ptycho.1 = (f32[2,512,512]{2,1,0:T(8,128)}, f32[2,2,256,256]{3,2,1,0:T(8,128)}) custom-call(s32[2,256]{1,0:T(2,128)} %bitcast.1, s32[128]{0:T(128)} %counts.1, f32[2,512,512]{2,1,0:T(8,128)} %obj_in.1, f32[2,2,256,256]{3,2,1,0:T(8,128)} %probe_in.1, f32[2,256,256]{2,1,0:T(8,128)} %meas_in.1, bf16[256,768]{1,0:T(8,128)(2,1)} %constant.16.clone.wl_in, ...), custom_call_target="tpu_custom_call" | custom-call | tf_op jit(solution)/shard_map/ptycho/pallas_call | solution.py:718
  192.6 0.0 copy-start
  192.6 3.2 %copy.17 = f32[2,512,512]{2,1,0:T(8,128)} copy(f32[2,512,512]{2,1,0:T(8,128)} %get-tuple-element.4) | data formatting | bytes 4194304
  195.7 0.0 copy-done
  195.8 1.0 copy.18
Async XLA Ops:
  192.6 3.2 %copy-start = (f32[2,2,256,256]{3,2,1,0:T(8,128)S(1)}, f32[2,2,256,256]{3,2,1,0:T(8,128)}, u32[]{:S(2)}) copy-start(f32[2,2,256,256]{3,2,1,0:T(8,128)} %get-tuple-element.5) | copy-start | bytes 3145732
where the time goes:
time: 197 us
  Pallas kernels  192 us (97%)
  local copies, waits for them, and re-layouts  4.14 us (2%)
    pallas_call x1, Pallas kernels, shards(): pl.pallas_call(functools.partial(kernel, rows_n, cols_n, nz, ny, streams)...  192 us
    unnamed x4, local copies, waits for them, and re-layouts  4.14 us

commit v1 on v0

--- a/solution.py
+++ b/solution.py
@@ -302,7 +302,8 @@
         root[s] = jnp.sqrt(value)
 
     for n, (ch, q) in enumerate(first):
-        pl.when(not_right)(lambda: to_left(obj, 0, ch, q).wait_recv())
+        with jax.named_scope("first_piece"):
+            pl.when(not_right)(lambda: to_left(obj, 0, ch, q).wait_recv())
         if n + 2 < len(first):
             first_piece(n + 2)
         for b in range(2):
@@ -488,17 +489,21 @@
 
     mode_sums, power_sum = (0, 1), (2,)
 
+    def zero_sums():
+        acc[...] = jnp.zeros_like(acc)
+        for n in range(3):
+            ar[13 * n][...] = jnp.zeros_like(ar[13 * n])
+
+    def take_all(it):
+        for s in range(2):
+            take(it, s)
+        ar_start(it, power_sum)
+
     def iteration(it, _):
         more = it < ITERS - 1
         send_left = not_left & more
         get_right = not_right & more
-        acc[...] = jnp.zeros_like(acc)
-        for n in range(3):
-            ar[13 * n][...] = jnp.zeros_like(ar[13 * n])
-
-        for s in range(2):
-            take(it, s)
-        ar_start(it, power_sum)
+        scope = jax.named_scope
 
         def one(s, carry):
             slot(it, s)
@@ -509,7 +514,8 @@
 
             return carry
 
-        lax.fori_loop(0, 2, one, 0)
+        with scope("slots"):
+            lax.fori_loop(0, 2, one, 0)
         ar_start(it, mode_sums)
 
         def send(ch, q):
@@ -537,6 +543,16 @@
                         step = acc[ch, 4 + b, rows, :] + hr[it + 1, ch, q, b, j:j + C, :]
                         obj[ch, 4 + b, there, :] += step * den[4 + b, rows, :]
 
+        def clear(it):
+            for ch in range(2):
+                for q in range(4):
+                    pl.when(not_right)(lambda: to_right(it, ch, q).wait_send())
+                    pl.when(send_left)(lambda: to_left(acc, it + 1, ch, q).wait_send())
+            for n in range(len(streams)):
+                for copy in phase_copies(it, n, 0):
+                    copy.wait_send()
+            zero_sums()
+
         def below(s, ch):
             pl.when(not_top)(lambda: down(it, s, ch).wait_recv())
             place(ch, -1, s, vu.at[it, s, ch])
@@ -547,75 +563,100 @@
             if ch == 0:
                 send(0, 2)
                 send(0, 3)
-        ar_step(it, power_sum, 1)
-        ar_step(it, mode_sums, 0)
-        for q in range(2):
-            if q == 0:
-                below(0, 0)
-                below(1, 0)
-            arrive(0, 2 + q)
-            send(0, q)
-        below(0, 1)
-        below(1, 1)
+        with scope("core_sums"):
+            ar_step(it, power_sum, 1)
+            ar_step(it, mode_sums, 0)
+        with scope("from_above"):
+            for q in range(2):
+                if q == 0:
+                    below(0, 0)
+                    below(1, 0)
+                arrive(0, 2 + q)
+                send(0, q)
+            below(0, 1)
+            below(1, 1)
         ar_step(it, power_sum, 2)
 
-        power_all = jnp.zeros((C, H), F32)
-        for b in range(2):
-            for i in range(0, M, C):
-                at = (slice(i, i + C), slice(b * H, b * H + H))
-                square = (
-                    probe[(0, 0) + at] ** 2 + probe[(1, 0) + at] ** 2
-                    + probe[(0, 1) + at] ** 2 + probe[(1, 1) + at] ** 2
-                )
-                power[b, i:i + C, :] = square
-                power_all = power_all + square
-        reg_object = DAMPING * (jnp.sum(power_all) * (1.0 / (M * M))) + SMALL
-        den[...] = jnp.zeros_like(den)
-        for dr in (0, -1):
-            for dc, blocks in ((0, range(6)), (-1, range(2)), (1, range(4, 6))):
-
-                def cover(s, carry, dr=dr, dc=dc, blocks=blocks):
-                    y, x, live = place_of(dr, dc, s)
-                    spread(cbuf, lambda i: (power[0, i:i + C, :], power[1, i:i + C, :]), x)
-                    add_placed(cbuf, den, blocks, dr, dc, y, x, live)
-                    return carry
-
-                lax.fori_loop(0, 2, cover, 0)
-        for b in range(6):
-            for i in range(0, T, C):
-                den[b, i:i + C, :] = 1.0 / (den[b, i:i + C, :] + reg_object)
-
-        arrive(0, 0)
+        with scope("coverage"):
+            power_all = jnp.zeros((C, H), F32)
+            for b in range(2):
+                for i in range(0, M, C):
+                    at = (slice(i, i + C), slice(b * H, b * H + H))
+                    square = (
+                        probe[(0, 0) + at] ** 2 + probe[(1, 0) + at] ** 2
+                        + probe[(0, 1) + at] ** 2 + probe[(1, 1) + at] ** 2
+                    )
+                    power[b, i:i + C, :] = square
+                    power_all = power_all + square
+            reg_object = DAMPING * (jnp.sum(power_all) * (1.0 / (M * M))) + SMALL
+            den[...] = jnp.zeros_like(den)
+            for dr in (0, -1):
+                for dc, blocks in ((0, range(6)), (-1, range(2)), (1, range(4, 6))):
+
+                    def cover(s, carry, dr=dr, dc=dc, blocks=blocks):
+                        y, x, live = place_of(dr, dc, s)
+                        spread(cbuf, lambda i: (power[0, i:i + C, :], power[1, i:i + C, :]), x)
+                        add_placed(cbuf, den, blocks, dr, dc, y, x, live)
+                        return carry
+
+                    lax.fori_loop(0, 2, cover, 0)
+            for b in range(6):
+                for i in range(0, T, C):
+                    den[b, i:i + C, :] = 1.0 / (den[b, i:i + C, :] + reg_object)
+
+        with scope("piece_00"):
+            arrive(0, 0)
         send(1, 0)
         update(0, 0)
-        ar_step(it, mode_sums, 1)
-        arrive(0, 1)
+        with scope("first_split"):
+            ar_step(it, mode_sums, 1)
+        with scope("piece_01"):
+            arrive(0, 1)
         send(1, 1)
         update(0, 1)
         pl.when(more)(lambda: send_up(it + 1, 0))
         ar_step(it, power_sum, 3)
-        ar_step(it, mode_sums, 2)
-        arrive(1, 0)
+        with scope("second_split"):
+            ar_step(it, mode_sums, 2)
+        with scope("piece_10"):
+            arrive(1, 0)
         send(1, 2)
         update(1, 0)
-        ar_step(it, mode_sums, 3)
-        arrive(1, 1)
+        with scope("exchange"):
+            ar_step(it, mode_sums, 3)
+        with scope("piece_11"):
+            arrive(1, 1)
         send(1, 3)
         update(1, 1)
         pl.when(more)(lambda: send_up(it + 1, 1))
         update(0, 2)
         update(0, 3)
         ar_step(it, power_sum, 4)
-        ar_step(it, mode_sums, 4)
-        arrive(1, 2)
+        with scope("first_gather"):
+            ar_step(it, mode_sums, 4)
+        with scope("piece_12"):
+            arrive(1, 2)
         update(1, 2)
         ar_step(it, power_sum, 5)
-        ar_step(it, mode_sums, 5)
-        arrive(1, 3)
+        with scope("piece_13"):
+            arrive(1, 3)
         update(1, 3)
-        for n in range(len(streams)):
-            for copy in phase_copies(it, n, 6):
-                copy.wait_recv()
+        clear(it)
+
+        @pl.when(more)
+        def _():
+            with scope("from_below"):
+                for ch in range(2):
+                    for s in range(2):
+                        pl.when(not_bottom)(lambda: up(it + 1, s, ch).wait_recv())
+            take_all(it + 1)
+
+        with scope("second_gather"):
+            ar_step(it, mode_sums, 5)
+        with scope("core_gather"):
+            for n in range(len(streams)):
+                for copy in phase_copies(it, n, 6):
+                    copy.wait_recv()
 
         def total(k, part, b, i):
             if k == 2:
@@ -636,16 +677,12 @@
                         probe[at] += total(k, part, b, i) * scale
 
         for n in range(len(streams)):
-            for phase in range(7):
+            for phase in range(1, 7):
                 for copy in phase_copies(it, n, phase):
                     copy.wait_send()
         for ch in range(2):
-            for q in range(4):
-                pl.when(not_right)(lambda: to_right(it, ch, q).wait_send())
-                pl.when(send_left)(lambda: to_left(acc, it + 1, ch, q).wait_send())
             for s in range(2):
                 pl.when(not_bottom)(lambda: down(it, s, ch).wait_send())
-                pl.when(not_bottom & more)(lambda: up(it + 1, s, ch).wait_recv())
                 pl.when(not_top & more)(lambda: up(it + 1, s, ch).wait_send())
         return 0
 
@@ -656,6 +693,8 @@
             pl.when(not_bottom)(lambda: up(0, s, ch).wait_recv())
             pl.when(not_top)(lambda: up(0, s, ch).wait_send())
 
+    zero_sums()
+    take_all(0)
     lax.fori_loop(0, ITERS, iteration, 0)
 
     stores = []

time: 197 us -> 195 us (0.990)
  Pallas kernels: 192 us -> 190 us
where the time goes in v1:
time: 195 us
  Pallas kernels  190 us (97%)
  local copies, waits for them, and re-layouts  4.14 us (2%)
    pallas_call x1, Pallas kernels, shards(): pl.pallas_call(functools.partial(kernel, rows_n, cols_n, nz, ny, streams)...  190 us
    unnamed x4, local copies, waits for them, and re-layouts  4.14 us

profile of v1, /device:TPU:1, one launch (start us, length us, event | category | flops | bytes accessed | tf_op | source)
XLA Modules:
  0.0 195.0 jit_solution(8058110847156675673)
XLA Ops:
  0.6 190.2 %ptycho.1 = (f32[2,512,512]{2,1,0:T(8,128)}, f32[2,2,256,256]{3,2,1,0:T(8,128)}) custom-call(s32[2,256]{1,0:T(2,128)} %bitcast.1, s32[128]{0:T(128)} %counts.1, f32[2,512,512]{2,1,0:T(8,128)} %obj_in.1, f32[2,2,256,256]{3,2,1,0:T(8,128)} %probe_in.1, f32[2,256,256]{2,1,0:T(8,128)} %meas_in.1, bf16[256,768]{1,0:T(8,128)(2,1)} %constant.16.clone.wl_in, ...), custom_call_target="tpu_custom_call" | custom-call | tf_op jit(solution)/shard_map/ptycho/pallas_call | solution.py:757
  190.8 0.0 copy-start
  190.8 3.2 %copy.17 = f32[2,512,512]{2,1,0:T(8,128)} copy(f32[2,512,512]{2,1,0:T(8,128)} %get-tuple-element.4) | data formatting | bytes 4194304
  194.0 0.0 copy-done
  194.0 1.0 copy.18
Async XLA Ops:
  190.8 3.2 %copy-start = (f32[2,2,256,256]{3,2,1,0:T(8,128)S(1)}, f32[2,2,256,256]{3,2,1,0:T(8,128)}, u32[]{:S(2)}) copy-start(f32[2,2,256,256]{3,2,1,0:T(8,128)} %get-tuple-element.5) | copy-start | bytes 3145732

commit v2 on v1

--- a/solution.py
+++ b/solution.py
@@ -519,8 +519,9 @@
         ar_start(it, mode_sums)
 
         def send(ch, q):
-            pl.when(not_right)(lambda: to_right(it, ch, q).start())
+            pl.when(not_right & (core == 0))(lambda: to_right(it, ch, q).start())
             pl.when(send_left)(lambda: to_left(acc, it + 1, ch, q).start())
+            pl.when(not_right & (core == 1))(lambda: to_right(it, ch, q).start())
 
         def arrive(ch, q):
             pl.when(not_left)(lambda: to_right(it, ch, q).wait_recv())

time: 195 us -> 196 us (level)
  no operation moved by 1% of the time
where the time goes in v2:
time: 196 us; the launch traced here: 195 us
  Pallas kernels  190 us (97%)
  local copies, waits for them, and re-layouts  4.14 us (2%)
    pallas_call x1, Pallas kernels, shards(): pl.pallas_call(functools.partial(kernel, rows_n, cols_n, nz, ny, streams)...  190 us
    unnamed x4, local copies, waits for them, and re-layouts  4.14 us

profile of v2, /device:TPU:1, one launch (start us, length us, event | category | flops | bytes accessed | tf_op | source)
XLA Modules:
  0.0 194.9 jit_solution(3464900261078153195)
XLA Ops:
  0.6 190.1 %ptycho.1 = (f32[2,512,512]{2,1,0:T(8,128)}, f32[2,2,256,256]{3,2,1,0:T(8,128)}) custom-call(s32[2,256]{1,0:T(2,128)} %bitcast.1, s32[128]{0:T(128)} %counts.1, f32[2,512,512]{2,1,0:T(8,128)} %obj_in.1, f32[2,2,256,256]{3,2,1,0:T(8,128)} %probe_in.1, f32[2,256,256]{2,1,0:T(8,128)} %meas_in.1, bf16[256,768]{1,0:T(8,128)(2,1)} %constant.16.clone.wl_in, ...), custom_call_target="tpu_custom_call" | custom-call | tf_op jit(solution)/shard_map/ptycho/pallas_call | solution.py:758
  190.8 0.0 copy-start
  190.8 3.2 %copy.17 = f32[2,512,512]{2,1,0:T(8,128)} copy(f32[2,512,512]{2,1,0:T(8,128)} %get-tuple-element.4) | data formatting | bytes 4194304
  193.9 0.0 copy-done
  193.9 1.0 copy.18
Async XLA Ops:
  190.8 3.2 %copy-start = (f32[2,2,256,256]{3,2,1,0:T(8,128)S(1)}, f32[2,2,256,256]{3,2,1,0:T(8,128)}, u32[]{:S(2)}) copy-start(f32[2,2,256,256]{3,2,1,0:T(8,128)} %get-tuple-element.5) | copy-start | bytes 3145732

commit v3 on v2

--- a/solution.py
+++ b/solution.py
@@ -576,6 +576,7 @@
                 send(0, q)
             below(0, 1)
             below(1, 1)
+        send(1, 0)
         ar_step(it, power_sum, 2)
 
         with scope("coverage"):
@@ -607,13 +608,13 @@
 
         with scope("piece_00"):
             arrive(0, 0)
-        send(1, 0)
+        send(1, 1)
         update(0, 0)
         with scope("first_split"):
             ar_step(it, mode_sums, 1)
         with scope("piece_01"):
             arrive(0, 1)
-        send(1, 1)
+        send(1, 2)
         update(0, 1)
         pl.when(more)(lambda: send_up(it + 1, 0))
         ar_step(it, power_sum, 3)
@@ -621,13 +622,12 @@
             ar_step(it, mode_sums, 2)
         with scope("piece_10"):
             arrive(1, 0)
-        send(1, 2)
+        send(1, 3)
         update(1, 0)
         with scope("exchange"):
             ar_step(it, mode_sums, 3)
         with scope("piece_11"):
             arrive(1, 1)
-        send(1, 3)
         update(1, 1)
         pl.when(more)(lambda: send_up(it + 1, 1))
         update(0, 2)

time: 196 us -> 201 us (1.026)
  Pallas kernels: 190 us -> 196 us
    pallas_call x1, Pallas kernels: 190 us -> 196 us  [shards(): pl.pallas_call(functools.partial(kernel, rows_n, cols_n, nz, ny, streams)...]
where the time goes in v3:
time: 201 us
  Pallas kernels  196 us (98%)
  local copies, waits for them, and re-layouts  4.14 us (2%)
    pallas_call x1, Pallas kernels, shards(): pl.pallas_call(functools.partial(kernel, rows_n, cols_n, nz, ny, streams)...  196 us
    unnamed x4, local copies, waits for them, and re-layouts  4.14 us

profile of v3, /device:TPU:1, one launch (start us, length us, event | category | flops | bytes accessed | tf_op | source)
XLA Modules:
  0.0 201.3 jit_solution(5616651743440083648)
XLA Ops:
  0.6 196.5 %ptycho.1 = (f32[2,512,512]{2,1,0:T(8,128)}, f32[2,2,256,256]{3,2,1,0:T(8,128)}) custom-call(s32[2,256]{1,0:T(2,128)} %bitcast.1, s32[128]{0:T(128)} %counts.1, f32[2,512,512]{2,1,0:T(8,128)} %obj_in.1, f32[2,2,256,256]{3,2,1,0:T(8,128)} %probe_in.1, f32[2,256,256]{2,1,0:T(8,128)} %meas_in.1, bf16[256,768]{1,0:T(8,128)(2,1)} %constant.16.clone.wl_in, ...), custom_call_target="tpu_custom_call" | custom-call | tf_op jit(solution)/shard_map/ptycho/pallas_call | solution.py:758
  197.1 0.0 copy-start
  197.1 3.2 %copy.17 = f32[2,512,512]{2,1,0:T(8,128)} copy(f32[2,512,512]{2,1,0:T(8,128)} %get-tuple-element.4) | data formatting | bytes 4194304
  200.3 0.0 copy-done
  200.3 1.0 copy.18
Async XLA Ops:
  197.1 3.2 %copy-start = (f32[2,2,256,256]{3,2,1,0:T(8,128)S(1)}, f32[2,2,256,256]{3,2,1,0:T(8,128)}, u32[]{:S(2)}) copy-start(f32[2,2,256,256]{3,2,1,0:T(8,128)} %get-tuple-element.5) | copy-start | bytes 3145732
